TPU v7x, 256 devices: a whole 4x4x8 slice. The times are simulated.
256 devices in a mesh: dp: 64 (over z, x, core), feat: 4 (over y).
Axes of the slice: x: 4, y: 4, z: 8, core: 2. Of those that a mesh axis runs over, the one named last changes fastest.
Arguments:
- member_feats: bfloat16 [262144, 256], P(('dp', 'feat')), may hold values from -6 to 6
- labels: int32 [262144], P(('dp', 'feat')), may hold values 0 or 1
- fixed_values: bfloat16 [262144, 2048], P('dp', 'feat'), may hold values from -6 to 6
- fixed_blocks: int32 [262144, 4], P('dp', 'feat'), may hold values from 0 to 511
- fixed_coef: float32 [2048, 512], P('feat'), may hold values from -0.12 to 0.12
- member_coef: float32 [1024, 256], P(('dp', 'feat')), may hold values from -0.36 to 0.36
- row_slot: int32 [262144], P(('dp', 'feat')), may hold values from 0 to 2047, as said below
- tile_source: int32 [622592], P(('dp', 'feat')), may hold values from 0 to 2048, as said below
- member_tiles: int32 [1024], P(('dp', 'feat')), may hold values from 1 to 16, as said below
Outputs:
- margin: float32 [262144], P(('dp', 'feat'))
- updated_coef: float32 [1024, 256], P(('dp', 'feat'))
- fixed_grad: float32 [2048, 512], P('feat')
Inputs may be any that keep to these rules, and one draw needn't show every extreme that they name: `row_slot`: each owner receives the same number of rows, 32, 16 or 8, from every device of its feat column; some owner receives 32 from every device. The rows one device sends to one owner take that owner's slots 0, 1, 2 and so on, each slot once. `tile_source`: every received row appears at exactly one position. An owner's members, in order, take consecutive runs of tiles; a member's rows fill its tiles from the first position on, and the rest of its last tile is padding, as are the tiles past all members. `member_tiles`: A member's tiles are its received rows divided by 128, rounded up; a device's members use at most 19 tiles in all, exactly 19 on the owners that receive 32 rows from every device.
All inputs are finite; a program needn't handle non-finite values. No bound on the sum of `labels` on one device may be relied on, other than what follows from the above.
Results may differ from a plain program's by a relative error of at most 0.0013.
Values may be sent and summed in bfloat16 or wider, within the bound.
A program may use at most 64 MiB of HBM per device.

v0:
```python
import functools

import jax
import jax.numpy as jnp
from jax import lax
from jax.experimental import pallas as pl
from jax.experimental.pallas import tpu as pltpu
from jax.sharding import PartitionSpec as P

CG_ITERS = 2
TILE = 128
LANES = 128
RIDGE_MEMBER = 1.0
RIDGE_FIXED = 1.0
F32 = jnp.float32
BF16 = jnp.bfloat16
MESH = pl.DeviceIdType.MESH


def dot_nn(a, b):
    return lax.dot_general(a, b, (((1,), (0,)), ((), ())), preferred_element_type=F32)


def dot_nt(a, b):
    return lax.dot_general(a, b, (((1,), (1,)), ((), ())), preferred_element_type=F32)


def dot_tn(a, b):
    return lax.dot_general(a, b, (((0,), (0,)), ((), ())), preferred_element_type=F32)


def split2(x):
    top = x.astype(BF16)
    return top, (x - top.astype(F32)).astype(BF16)


def iota(shape, dim):
    return lax.broadcasted_iota(jnp.int32, shape, dim)


def as_bf16(mask):
    return jnp.where(mask, 1.0, 0.0).astype(BF16)


def as_f32(mask):
    return jnp.where(mask, 1.0, 0.0).astype(F32)


def grid_of(dp):
    return (8, 4, 2) if dp == 64 else (dp // 4, 2, 2)


def kernel(
    dp,
    feat,
    cap,
    feats,
    labels,
    fv,
    fb,
    fc,
    mcoef,
    rslot,
    tsrc,
    mtiles,
    margin_out,
    coef_out,
    grad_out,
    send_x,
    recv_x,
    send_p,
    recv_p,
    send_s,
    recv_s,
    send_r,
    recv_r,
    send_e,
    recv_e,
    coef_parts,
    member_mask,
    acc,
    recv_c,
    recv_rx,
    recv_rz,
    sx,
    rx,
    sp,
    rp,
    ss,
    rs,
    sr,
    rr,
    se,
    re,
    sc,
    rc,
    srx,
    rrx,
    srz,
    rrz,
    sgz,
    rgz,
    sgx,
    rgx,
    sgc,
    rgc,
):
    planes, chips, cores = grid_of(dp)
    rows = feats.shape[0]
    slots = dp * cap
    cap_bits = cap.bit_length() - 1
    block_count, block_width = fc.shape
    plane_owners = chips * cores
    plane_slots = plane_owners * cap
    i = lax.axis_index("dp")
    f = lax.axis_index("feat")
    z = i // plane_owners
    x = (i % plane_owners) // cores
    c = i % cores

    def at(dp_index, feat_index=None):
        return (dp_index, f if feat_index is None else feat_index)

    barrier = pltpu.get_barrier_semaphore()

    def greet_dp(k, carry):
        pl.semaphore_signal(barrier, inc=1, device_id=at((i + k) % dp), device_id_type=MESH)
        return carry

    lax.fori_loop(1, dp, greet_dp, 0)
    for k in range(1, feat):
        pl.semaphore_signal(
            barrier, inc=1, device_id=at(i, (f + k) % feat), device_id_type=MESH
        )
    pl.semaphore_wait(barrier, dp - 1 + feat - 1)

    slot_row = rslot[...]
    feats_here = feats[...]

    def send_plane(k, carry):
        plane = (z + k) % planes
        base = plane * plane_slots
        pick = as_bf16(slot_row - base == iota((plane_slots, rows), 0))
        picked = dot_nn(pick, feats_here).astype(BF16)
        send_x[pl.ds(plane * plane_owners, plane_owners)] = picked.reshape(
            plane_owners, cap, feats.shape[1]
        )

        def send_owner(q, inner):
            owner = plane * plane_owners + (i + q) % plane_owners

            @pl.when(owner != i)
            def _():
                pltpu.make_async_remote_copy(
                    src_ref=send_x.at[owner],
                    dst_ref=recv_x.at[i],
                    send_sem=sx,
                    recv_sem=rx,
                    device_id=at(owner),
                    device_id_type=MESH,
                ).start()

            return inner

        return lax.fori_loop(0, plane_owners, send_owner, carry)

    lax.fori_loop(0, planes, send_plane, 0)
    recv_x[i] = send_x[i]

    group_rows = feat * rows
    step = min(512, rows)
    coef_parts[0], coef_parts[1] = split2(fc[...])

    def partial_chunk(q, carry):
        start = pl.multiple_of(q * step, step)
        values = fv[pl.ds(start, step), :]
        scores = dot_nt(coef_parts[0], values) + dot_nt(coef_parts[1], values)
        hot = fb[:, pl.ds(start, step)] == iota((block_count, step), 0)
        part = jnp.sum(jnp.where(hot, scores, 0.0), axis=0, keepdims=True)
        per = rows // step
        inner = pl.multiple_of((q % per) * step, step)
        send_p[q // per, :, pl.ds(inner, step)] = part
        return carry

    lax.fori_loop(0, group_rows // step, partial_chunk, 0)
    for k in range(1, feat):
        other = (f + k) % feat
        pltpu.make_async_remote_copy(
            src_ref=send_p.at[other],
            dst_ref=recv_p.at[f],
            send_sem=sp,
            recv_sem=rp,
            device_id=at(i, other),
            device_id_type=MESH,
        ).start()
    recv_p[f] = send_p[f]

    positions = tsrc.shape[1]
    tile = iota((1, positions), 1) >> (TILE.bit_length() - 1)
    members = mcoef.shape[0]
    member = jnp.zeros((1, positions), jnp.int32)
    end = jnp.int32(0)
    for m in range(members):
        end = end + mtiles[m]
        member = member + jnp.where(tile >= end, 1, 0)
    source = tsrc[...]
    code = (member << cap_bits) + (source & (cap - 1))
    code_hot = as_bf16(code == iota((members * cap, positions), 0))
    sender_hot = as_bf16((source >> cap_bits) == iota((dp, positions), 0))
    counted = dot_nt(code_hot, sender_hot).astype(BF16)
    spread = as_bf16((iota((dp, slots), 1) >> cap_bits) == iota((dp, slots), 0))
    slot_mask = as_f32((iota((cap, slots), 1) & (cap - 1)) == iota((cap, slots), 0))
    widened = dot_nn(counted, spread)
    for m in range(members):
        member_mask[pl.ds(m, 1), :] = jnp.sum(
            widened[m * cap : (m + 1) * cap] * slot_mask, axis=0, keepdims=True
        )

    owner_hot = as_bf16((slot_row >> cap_bits) == iota((dp, rows), 0))
    slot_hot = as_f32((slot_row & (cap - 1)) == iota((cap, rows), 0))
    label_row = labels[...].astype(F32)
    zeros_row = jnp.zeros((LANES - 2 * cap, rows), BF16)

    def wait_all(ref, sem):
        pltpu.make_async_copy(ref, ref, sem).wait()

    wait_all(recv_p.at[pl.ds(0, feat - 1)], rp)
    fixed_score = recv_p[0]
    for k in range(1, feat):
        fixed_score = fixed_score + recv_p[k]

    sent = fixed_score.astype(BF16).astype(F32)
    payload = jnp.concatenate(
        [(slot_hot * sent).astype(BF16), (slot_hot * label_row).astype(BF16), zeros_row], axis=0
    )
    scattered = dot_nt(owner_hot, payload)
    send_s[...] = scattered.reshape(dp, 1, LANES)

    def send_score(k, carry):
        owner = (i + k) % dp
        pltpu.make_async_remote_copy(
            src_ref=send_s.at[owner],
            dst_ref=recv_s.at[i],
            send_sem=ss,
            recv_sem=rs,
            device_id=at(owner),
            device_id_type=MESH,
        ).start()
        return carry

    lax.fori_loop(1, dp, send_score, 0)
    recv_s[i] = send_s[i]
    wait_all(recv_x.at[pl.ds(0, dp - 1)], rx)
    wait_all(recv_s.at[pl.ds(0, dp - 1)], rs)

    mask = member_mask[...]
    got = recv_x[...].reshape(slots, feats.shape[1])
    arrived = recv_s[...].reshape(dp, LANES)[:, : 2 * cap].astype(BF16)
    expanded = dot_tn(arrived, spread)
    score_row = jnp.sum(expanded[:cap] * slot_mask, axis=0, keepdims=True)
    answer_row = jnp.sum(expanded[cap:] * slot_mask, axis=0, keepdims=True)

    def project(vectors):
        top, low = split2(vectors)
        dots = dot_nt(jnp.concatenate([top, low], axis=0), got)
        return jnp.sum((dots[:members] + dots[members:]) * mask, axis=0, keepdims=True)

    def gather_rows(weights):
        top, low = split2(mask * weights)
        sums = dot_nn(jnp.concatenate([top, low], axis=0), got)
        return sums[:members] + sums[members:]

    coef = mcoef[...]
    probability = 1.0 / (1.0 + jnp.exp(-(score_row + project(coef))))
    weight = probability * (1.0 - probability)
    gradient = gather_rows(answer_row - probability) - RIDGE_MEMBER * coef
    got_wide = got.astype(F32)
    square_top, square_low = split2(got_wide * got_wide)
    weight_top, weight_low = split2(mask * weight)
    first = dot_nn(jnp.concatenate([weight_top, weight_low], axis=0), square_top)
    second = dot_nn(weight_top, square_low)
    diagonal = first[:members] + first[members:] + second + RIDGE_MEMBER
    step_sum = jnp.zeros_like(coef)
    remain = gradient
    scaled = remain / diagonal
    search = scaled
    inner_product = jnp.sum(remain * scaled, axis=1, keepdims=True)
    for iteration in range(CG_ITERS):
        image = gather_rows(weight * project(search)) + RIDGE_MEMBER * search
        alpha = inner_product / jnp.sum(search * image, axis=1, keepdims=True)
        step_sum = step_sum + alpha * search
        if iteration + 1 < CG_ITERS:
            remain = remain - alpha * image
            scaled = remain / diagonal
            inner_next = jnp.sum(remain * scaled, axis=1, keepdims=True)
            search = scaled + (inner_next / inner_product) * search
            inner_product = inner_next
    updated = coef + step_sum
    coef_out[...] = updated

    new_top, new_low = split2(project(updated))
    stacked = jnp.concatenate([spread * new_top, spread * new_low], axis=0)
    slot_wide = as_bf16((iota((LANES, slots), 1) & (cap - 1)) == iota((LANES, slots), 0))
    folded = dot_nt(stacked, slot_wide)
    send_r[...] = (folded[:dp] + folded[dp:]).reshape(dp, 1, LANES)

    def send_back(k, carry):
        sender = (i + k) % dp
        pltpu.make_async_remote_copy(
            src_ref=send_r.at[sender],
            dst_ref=recv_r.at[i],
            send_sem=sr,
            recv_sem=rr,
            device_id=at(sender),
            device_id_type=MESH,
        ).start()
        return carry

    lax.fori_loop(1, dp, send_back, 0)
    recv_r[i] = send_r[i]
    wait_all(recv_r.at[pl.ds(0, dp - 1)], rr)
    back_top, back_low = split2(recv_r[...].reshape(dp, LANES)[:, :cap])
    looked = dot_tn(back_top, owner_hot) + dot_tn(back_low, owner_hot)
    member_score = jnp.sum(looked * slot_hot, axis=0, keepdims=True)
    margin = fixed_score + member_score
    margin_out[...] = margin
    send_e[...] = label_row - 1.0 / (1.0 + jnp.exp(-margin))
    for k in range(1, feat):
        other = (f + k) % feat
        pltpu.make_async_remote_copy(
            src_ref=send_e,
            dst_ref=recv_e.at[f],
            send_sem=se.at[k - 1],
            recv_sem=re,
            device_id=at(i, other),
            device_id_type=MESH,
        ).start()
    recv_e[f] = send_e[...]
    wait_all(recv_e.at[pl.ds(0, feat - 1)], re)

    half = block_count // cores
    piece = half // 2

    def gradient_rows(start):
        def add_chunk(q, total):
            first_row = pl.multiple_of(q * step, step)
            values = fv[pl.ds(first_row, step), :]
            per = rows // step
            inner = pl.multiple_of((q % per) * step, step)
            left = recv_e[q // per, :, pl.ds(inner, step)]
            hot = fb[:, pl.ds(first_row, step)] - start == iota((piece, step), 0)
            weighted = jnp.where(hot, left, 0.0)
            top, low = split2(weighted)
            return total + dot_nn(top, values) + dot_nn(low, values)

        acc[pl.ds(start, piece), :] = lax.fori_loop(
            0, group_rows // step, add_chunk, jnp.zeros((piece, block_width), F32)
        )

    partner = z * plane_owners + x * cores + (1 - c)
    theirs = (1 - c) * half
    core_copies = []
    for k in range(2):
        start = pl.multiple_of(theirs + k * piece, piece)
        gradient_rows(start)
        copy = pltpu.make_async_remote_copy(
            src_ref=acc.at[pl.ds(start, piece)],
            dst_ref=recv_c.at[pl.ds(k * piece, piece)],
            send_sem=sc.at[k],
            recv_sem=rc.at[k],
            device_id=at(partner),
            device_id_type=MESH,
        )
        copy.start()
        core_copies.append(copy)
    mine = pl.multiple_of(c * half, half)
    for k in range(2):
        gradient_rows(pl.multiple_of(mine + k * piece, piece))
    for copy in core_copies:
        copy.wait_recv()
    acc[pl.ds(mine, half), :] = acc[pl.ds(mine, half), :] + recv_c[...]

    strip = half // chips
    share = strip // planes

    def along_x(k):
        return (x + k) % chips

    def along_z(k):
        return (z + k) % planes

    for k in range(1, chips):
        other = along_x(k)
        pltpu.make_async_remote_copy(
            src_ref=acc.at[pl.ds(pl.multiple_of(mine + other * strip, strip), strip)],
            dst_ref=recv_rx.at[x],
            send_sem=srx,
            recv_sem=rrx,
            device_id=at(z * plane_owners + other * cores + c),
            device_id_type=MESH,
        ).start()
    my_strip = pl.multiple_of(mine + x * strip, strip)
    recv_rx[x] = acc[pl.ds(my_strip, strip), :]
    wait_all(recv_rx.at[pl.ds(0, chips - 1)], rrx)
    total = recv_rx[0]
    for k in range(1, chips):
        total = total + recv_rx[k]
    acc[pl.ds(my_strip, strip), :] = total
    for k in range(1, planes):
        other = along_z(k)
        pltpu.make_async_remote_copy(
            src_ref=acc.at[pl.ds(pl.multiple_of(my_strip + other * share, share), share)],
            dst_ref=recv_rz.at[z],
            send_sem=srz,
            recv_sem=rrz,
            device_id=at(other * plane_owners + x * cores + c),
            device_id_type=MESH,
        ).start()
    my_share = pl.multiple_of(my_strip + z * share, share)
    recv_rz[z] = acc[pl.ds(my_share, share), :]
    wait_all(recv_rz.at[pl.ds(0, planes - 1)], rrz)
    total = recv_rz[0]
    for k in range(1, planes):
        total = total + recv_rz[k]
    grad_out[pl.ds(my_share, share), :] = (
        RIDGE_FIXED * fc[pl.ds(my_share, share), :] - total / dp
    )

    for k in range(1, planes):
        pltpu.make_async_remote_copy(
            src_ref=grad_out.at[pl.ds(my_share, share)],
            dst_ref=grad_out.at[pl.ds(my_share, share)],
            send_sem=sgz,
            recv_sem=rgz,
            device_id=at(along_z(k) * plane_owners + x * cores + c),
            device_id_type=MESH,
        ).start()
    wait_all(grad_out.at[pl.ds(0, (planes - 1) * share)], rgz)
    for k in range(1, chips):
        pltpu.make_async_remote_copy(
            src_ref=grad_out.at[pl.ds(my_strip, strip)],
            dst_ref=grad_out.at[pl.ds(my_strip, strip)],
            send_sem=sgx,
            recv_sem=rgx,
            device_id=at(z * plane_owners + along_x(k) * cores + c),
            device_id_type=MESH,
        ).start()
    wait_all(grad_out.at[pl.ds(0, (chips - 1) * strip)], rgx)
    last = pltpu.make_async_remote_copy(
        src_ref=grad_out.at[pl.ds(mine, half)],
        dst_ref=grad_out.at[pl.ds(mine, half)],
        send_sem=sgc,
        recv_sem=rgc,
        device_id=at(partner),
        device_id_type=MESH,
    )
    last.start()
    last.wait()

    wait_all(send_x.at[pl.ds(0, dp - 1)], sx)
    wait_all(send_p.at[pl.ds(0, feat - 1)], sp)
    wait_all(send_s.at[pl.ds(0, dp - 1)], ss)
    wait_all(send_r.at[pl.ds(0, dp - 1)], sr)
    for k in range(1, feat):
        wait_all(send_e, se.at[k - 1])
    for copy in core_copies:
        copy.wait_send()
    wait_all(recv_rx.at[pl.ds(0, chips - 1)], srx)
    wait_all(recv_rz.at[pl.ds(0, planes - 1)], srz)
    wait_all(grad_out.at[pl.ds(0, (planes - 1) * share)], sgz)
    wait_all(grad_out.at[pl.ds(0, (chips - 1) * strip)], sgx)


def body(
    member_feats,
    labels,
    fixed_values,
    fixed_blocks,
    fixed_coef,
    member_coef,
    row_slot,
    tile_source,
    member_tiles,
):
    dp = lax.axis_size("dp")
    feat = lax.axis_size("feat")
    planes, chips, cores = grid_of(dp)
    rows, width = member_feats.shape
    members = member_coef.shape[0]
    block_count, block_width = fixed_coef.shape
    cap = 2 * rows // dp
    half = block_count // cores
    vmem = pl.BlockSpec(memory_space=pltpu.VMEM)
    smem = pl.BlockSpec(memory_space=pltpu.SMEM)
    dma = pltpu.SemaphoreType.DMA
    margin, updated, grad = pl.pallas_call(
        functools.partial(kernel, dp, feat, cap),
        out_shape=(
            jax.ShapeDtypeStruct((1, rows), F32),
            jax.ShapeDtypeStruct((members, width), F32),
            jax.ShapeDtypeStruct((block_count, block_width), F32),
        ),
        in_specs=[vmem] * 8 + [smem],
        out_specs=(vmem, vmem, vmem),
        scratch_shapes=[
            pltpu.VMEM((dp, cap, width), BF16),
            pltpu.VMEM((dp, cap, width), BF16),
            pltpu.VMEM((feat, 1, rows), F32),
            pltpu.VMEM((feat, 1, rows), F32),
            pltpu.VMEM((dp, 1, LANES), F32),
            pltpu.VMEM((dp, 1, LANES), F32),
            pltpu.VMEM((dp, 1, LANES), F32),
            pltpu.VMEM((dp, 1, LANES), F32),
            pltpu.VMEM((1, rows), F32),
            pltpu.VMEM((feat, 1, rows), F32),
            pltpu.VMEM((2, block_count, block_width), BF16),
            pltpu.VMEM((members, dp * cap), F32),
            pltpu.VMEM((block_count, block_width), F32),
            pltpu.VMEM((half, block_width), F32),
            pltpu.VMEM((chips, half // chips, block_width), F32),
            pltpu.VMEM((planes, half // chips // planes, block_width), F32),
            dma,
            dma,
            dma,
            dma,
            dma,
            dma,
            dma,
            dma,
            dma((feat - 1,)),
            dma,
            dma((2,)),
            dma((2,)),
            dma,
            dma,
            dma,
            dma,
            dma,
            dma,
            dma,
            dma,
            dma,
            dma,
        ],
        compiler_params=pltpu.CompilerParams(
            collective_id=0, has_side_effects=True, vmem_limit_bytes=56 * 2**20
        ),
    )(
        member_feats,
        labels.reshape(1, rows),
        fixed_values,
        fixed_blocks.reshape(1, feat * rows),
        fixed_coef,
        member_coef,
        row_slot.reshape(1, rows),
        tile_source.reshape(1, -1),
        member_tiles,
    )
    return margin.reshape(rows), updated, grad


def solution(mesh):
    placed = (
        P(("dp", "feat"), None),
        P(("dp", "feat")),
        P("dp", "feat"),
        P("dp", "feat"),
        P("feat", None),
        P(("dp", "feat"), None),
        P(("dp", "feat")),
        P(("dp", "feat")),
        P(("dp", "feat")),
    )
    return jax.shard_map(
        body,
        mesh=mesh,
        in_specs=placed,
        out_specs=(P(("dp", "feat")), P(("dp", "feat"), None), P("feat", None)),
        check_vma=False,
    )
```

profile of v0, /device:TPU:1, one launch (start us, length us, event | category | flops | bytes accessed | tf_op | source)
XLA Modules:
  0.0 104.4 jit_solution(1732973592858015610)
XLA Ops:
  0.6 1.3 %reshape.24.tsrc = s32[1,2432]{1,0:T(1,128)} reshape(s32[2432]{0:T(1024)} %param.16) | data formatting | bytes 19456 | tf_op jit(solution)/shard_map/reshape | solution.py:556
  1.9 97.7 %shard_map.112 = (f32[1,1024]{1,0:T(1,128)}, f32[4,256]{1,0:T(4,128)}, f32[512,512]{1,0:T(8,128)}) custom-call(bf16[1024,256]{1,0:T(8,128)(2,1)} %feats.1, s32[1,1024]{1,0:T(1,128)} %bitcast.5, bf16[4096,512]{1,0:T(8,128)(2,1)} %fv.1, s32[1,4096]{1,0:T(1,128)} %bitcast.4, f32[512,512]{1,0:T(8,128)} %fc.1, f32[4,256]{1,0:T(4,128)} %mcoef.1, ...), custom_call_target="tpu_custom_call" | custom-call | tf_op jit(solution)/shard_map/pallas_call | solution.py:496
  99.6 1.3 %copy.15 = f32[1024]{0:T(1024)} copy(f32[1024]{0:T(1024)} %bitcast.7) | data formatting | bytes 8192
  100.9 1.3 %copy.16 = f32[4,256]{1,0:T(4,128)} copy(f32[4,256]{1,0:T(4,128)} %get-tuple-element.13) | data formatting | bytes 8192
  102.2 2.3 %copy.17 = f32[512,512]{1,0:T(8,128)} copy(f32[512,512]{1,0:T(8,128)} %get-tuple-element.14) | data formatting | bytes 2097152
where the time goes:
time: 105 us; the launch traced here: 104 us
  Pallas kernels  97.7 us (93%)
  local copies, waits for them, and re-layouts  6.11 us (6%)
    pallas_call x1, Pallas kernels, body(): pl.pallas_call(functools.partial(kernel, dp, feat, cap), out_shape=(jax.S...  97.7 us
    unnamed x3, local copies, waits for them, and re-layouts  4.8 us

commit v1 on v0

--- a/solution.py
+++ b/solution.py
@@ -54,11 +54,11 @@
     dp,
     feat,
     cap,
-    feats,
+    feats_hbm,
     labels,
-    fv,
+    fv_hbm,
     fb,
-    fc,
+    fc_hbm,
     mcoef,
     rslot,
     tsrc,
@@ -66,6 +66,10 @@
     margin_out,
     coef_out,
     grad_out,
+    feats,
+    fv,
+    fc,
+    hot_all,
     send_x,
     recv_x,
     send_p,
@@ -104,6 +108,7 @@
     rgx,
     sgc,
     rgc,
+    s_load,
 ):
     planes, chips, cores = grid_of(dp)
     rows = feats.shape[0]
@@ -121,6 +126,16 @@
     def at(dp_index, feat_index=None):
         return (dp_index, f if feat_index is None else feat_index)
 
+    def wait_all(ref, sem):
+        pltpu.make_async_copy(ref, ref, sem).wait()
+
+    loads = [
+        pltpu.make_async_copy(source, target, s_load.at[k])
+        for k, (source, target) in enumerate(((feats_hbm, feats), (fc_hbm, fc), (fv_hbm, fv)))
+    ]
+    for load in loads:
+        load.start()
+
     barrier = pltpu.get_barrier_semaphore()
 
     def greet_dp(k, carry):
@@ -132,51 +147,62 @@
         pl.semaphore_signal(
             barrier, inc=1, device_id=at(i, (f + k) % feat), device_id_type=MESH
         )
-    pl.semaphore_wait(barrier, dp - 1 + feat - 1)
 
     slot_row = rslot[...]
+    loads[0].wait()
     feats_here = feats[...]
 
-    def send_plane(k, carry):
-        plane = (z + k) % planes
+    def pick_plane(plane, carry):
         base = plane * plane_slots
         pick = as_bf16(slot_row - base == iota((plane_slots, rows), 0))
         picked = dot_nn(pick, feats_here).astype(BF16)
         send_x[pl.ds(plane * plane_owners, plane_owners)] = picked.reshape(
             plane_owners, cap, feats.shape[1]
         )
-
-        def send_owner(q, inner):
-            owner = plane * plane_owners + (i + q) % plane_owners
-
-            @pl.when(owner != i)
-            def _():
-                pltpu.make_async_remote_copy(
-                    src_ref=send_x.at[owner],
-                    dst_ref=recv_x.at[i],
-                    send_sem=sx,
-                    recv_sem=rx,
-                    device_id=at(owner),
-                    device_id_type=MESH,
-                ).start()
-
-            return inner
-
-        return lax.fori_loop(0, plane_owners, send_owner, carry)
-
-    lax.fori_loop(0, planes, send_plane, 0)
+        return carry
+
+    lax.fori_loop(0, planes, pick_plane, 0)
+    pl.semaphore_wait(barrier, dp - 1 + feat - 1)
+
+    def send_feats(owner):
+        pltpu.make_async_remote_copy(
+            src_ref=send_x.at[owner],
+            dst_ref=recv_x.at[i],
+            send_sem=sx,
+            recv_sem=rx,
+            device_id=at(owner),
+            device_id_type=MESH,
+        ).start()
+
+    def send_far(q, carry):
+        for k in sorted(range(1, planes), key=lambda k: -min(k, planes - k)):
+            send_feats(((z + k) % planes) * plane_owners + (i + q) % plane_owners)
+        return carry
+
+    def send_near(q, carry):
+        send_feats(z * plane_owners + (i + q) % plane_owners)
+        return carry
+
+    lax.fori_loop(0, plane_owners, send_far, 0)
+    lax.fori_loop(1, plane_owners, send_near, 0)
     recv_x[i] = send_x[i]
 
     group_rows = feat * rows
     step = min(512, rows)
-    coef_parts[0], coef_parts[1] = split2(fc[...])
+    loads[1].wait()
+    coef_top, coef_low = split2(fc[...])
+    coef_parts[:block_count] = coef_top
+    coef_parts[block_count:] = coef_low
+    loads[2].wait()
 
     def partial_chunk(q, carry):
         start = pl.multiple_of(q * step, step)
         values = fv[pl.ds(start, step), :]
-        scores = dot_nt(coef_parts[0], values) + dot_nt(coef_parts[1], values)
-        hot = fb[:, pl.ds(start, step)] == iota((block_count, step), 0)
-        part = jnp.sum(jnp.where(hot, scores, 0.0), axis=0, keepdims=True)
+        scores = dot_nt(coef_parts[...], values)
+        scores = scores[:block_count] + scores[block_count:]
+        hot = as_f32(fb[:, pl.ds(start, step)] == iota((block_count, step), 0))
+        hot_all[:, pl.ds(start, step)] = hot.astype(BF16)
+        part = jnp.sum(scores * hot, axis=0, keepdims=True)
         per = rows // step
         inner = pl.multiple_of((q % per) * step, step)
         send_p[q // per, :, pl.ds(inner, step)] = part
@@ -195,7 +221,7 @@
         ).start()
     recv_p[f] = send_p[f]
 
-    positions = tsrc.shape[1]
+    positions = tsrc.shape[0]
     tile = iota((1, positions), 1) >> (TILE.bit_length() - 1)
     members = mcoef.shape[0]
     member = jnp.zeros((1, positions), jnp.int32)
@@ -203,7 +229,7 @@
     for m in range(members):
         end = end + mtiles[m]
         member = member + jnp.where(tile >= end, 1, 0)
-    source = tsrc[...]
+    source = tsrc[...].reshape(1, positions)
     code = (member << cap_bits) + (source & (cap - 1))
     code_hot = as_bf16(code == iota((members * cap, positions), 0))
     sender_hot = as_bf16((source >> cap_bits) == iota((dp, positions), 0))
@@ -220,9 +246,6 @@
     slot_hot = as_f32((slot_row & (cap - 1)) == iota((cap, rows), 0))
     label_row = labels[...].astype(F32)
     zeros_row = jnp.zeros((LANES - 2 * cap, rows), BF16)
-
-    def wait_all(ref, sem):
-        pltpu.make_async_copy(ref, ref, sem).wait()
 
     wait_all(recv_p.at[pl.ds(0, feat - 1)], rp)
     fixed_score = recv_p[0]
@@ -339,45 +362,37 @@
     wait_all(recv_e.at[pl.ds(0, feat - 1)], re)
 
     half = block_count // cores
-    piece = half // 2
 
     def gradient_rows(start):
         def add_chunk(q, total):
             first_row = pl.multiple_of(q * step, step)
-            values = fv[pl.ds(first_row, step), :]
             per = rows // step
             inner = pl.multiple_of((q % per) * step, step)
-            left = recv_e[q // per, :, pl.ds(inner, step)]
-            hot = fb[:, pl.ds(first_row, step)] - start == iota((piece, step), 0)
-            weighted = jnp.where(hot, left, 0.0)
-            top, low = split2(weighted)
-            return total + dot_nn(top, values) + dot_nn(low, values)
-
-        acc[pl.ds(start, piece), :] = lax.fori_loop(
-            0, group_rows // step, add_chunk, jnp.zeros((piece, block_width), F32)
+            top, low = split2(recv_e[q // per, :, pl.ds(inner, step)])
+            hot = hot_all[pl.ds(start, half), pl.ds(first_row, step)]
+            weighted = jnp.concatenate([hot * top, hot * low], axis=0)
+            return total + dot_nn(weighted, fv[pl.ds(first_row, step), :])
+
+        total = lax.fori_loop(
+            0, group_rows // step, add_chunk, jnp.zeros((2 * half, block_width), F32)
         )
+        acc[pl.ds(start, half), :] = total[:half] + total[half:]
 
     partner = z * plane_owners + x * cores + (1 - c)
-    theirs = (1 - c) * half
-    core_copies = []
-    for k in range(2):
-        start = pl.multiple_of(theirs + k * piece, piece)
-        gradient_rows(start)
-        copy = pltpu.make_async_remote_copy(
-            src_ref=acc.at[pl.ds(start, piece)],
-            dst_ref=recv_c.at[pl.ds(k * piece, piece)],
-            send_sem=sc.at[k],
-            recv_sem=rc.at[k],
-            device_id=at(partner),
-            device_id_type=MESH,
-        )
-        copy.start()
-        core_copies.append(copy)
+    theirs = pl.multiple_of((1 - c) * half, half)
     mine = pl.multiple_of(c * half, half)
-    for k in range(2):
-        gradient_rows(pl.multiple_of(mine + k * piece, piece))
-    for copy in core_copies:
-        copy.wait_recv()
+    gradient_rows(theirs)
+    core_copy = pltpu.make_async_remote_copy(
+        src_ref=acc.at[pl.ds(theirs, half)],
+        dst_ref=recv_c,
+        send_sem=sc,
+        recv_sem=rc,
+        device_id=at(partner),
+        device_id_type=MESH,
+    )
+    core_copy.start()
+    gradient_rows(mine)
+    core_copy.wait_recv()
     acc[pl.ds(mine, half), :] = acc[pl.ds(mine, half), :] + recv_c[...]
 
     strip = half // chips
@@ -463,12 +478,24 @@
     wait_all(send_r.at[pl.ds(0, dp - 1)], sr)
     for k in range(1, feat):
         wait_all(send_e, se.at[k - 1])
-    for copy in core_copies:
-        copy.wait_send()
+    core_copy.wait_send()
     wait_all(recv_rx.at[pl.ds(0, chips - 1)], srx)
     wait_all(recv_rz.at[pl.ds(0, planes - 1)], srz)
     wait_all(grad_out.at[pl.ds(0, (planes - 1) * share)], sgz)
     wait_all(grad_out.at[pl.ds(0, (chips - 1) * strip)], sgx)
+
+
+def hand_over(margin, updated, grad, margin_out, updated_out, grad_out, sems):
+    copies = [
+        pltpu.make_async_copy(source, target, sems.at[k])
+        for k, (source, target) in enumerate(
+            ((grad, grad_out), (updated, updated_out), (margin, margin_out))
+        )
+    ]
+    for copy in copies:
+        copy.start()
+    for copy in copies:
+        copy.wait()
 
 
 def body(
@@ -491,6 +518,7 @@
     cap = 2 * rows // dp
     half = block_count // cores
     vmem = pl.BlockSpec(memory_space=pltpu.VMEM)
+    hbm = pl.BlockSpec(memory_space=pl.ANY)
     smem = pl.BlockSpec(memory_space=pltpu.SMEM)
     dma = pltpu.SemaphoreType.DMA
     margin, updated, grad = pl.pallas_call(
@@ -500,9 +528,13 @@
             jax.ShapeDtypeStruct((members, width), F32),
             jax.ShapeDtypeStruct((block_count, block_width), F32),
         ),
-        in_specs=[vmem] * 8 + [smem],
+        in_specs=[hbm, vmem, hbm, vmem, hbm, vmem, vmem, vmem, smem],
         out_specs=(vmem, vmem, vmem),
         scratch_shapes=[
+            pltpu.VMEM((rows, width), BF16),
+            pltpu.VMEM(fixed_values.shape, BF16),
+            pltpu.VMEM((block_count, block_width), F32),
+            pltpu.VMEM((block_count, feat * rows), BF16),
             pltpu.VMEM((dp, cap, width), BF16),
             pltpu.VMEM((dp, cap, width), BF16),
             pltpu.VMEM((feat, 1, rows), F32),
@@ -513,7 +545,7 @@
             pltpu.VMEM((dp, 1, LANES), F32),
             pltpu.VMEM((1, rows), F32),
             pltpu.VMEM((feat, 1, rows), F32),
-            pltpu.VMEM((2, block_count, block_width), BF16),
+            pltpu.VMEM((2 * block_count, block_width), BF16),
             pltpu.VMEM((members, dp * cap), F32),
             pltpu.VMEM((block_count, block_width), F32),
             pltpu.VMEM((half, block_width), F32),
@@ -529,18 +561,19 @@
             dma,
             dma((feat - 1,)),
             dma,
-            dma((2,)),
-            dma((2,)),
-            dma,
-            dma,
-            dma,
-            dma,
-            dma,
-            dma,
-            dma,
-            dma,
-            dma,
-            dma,
+            dma,
+            dma,
+            dma,
+            dma,
+            dma,
+            dma,
+            dma,
+            dma,
+            dma,
+            dma,
+            dma,
+            dma,
+            dma((3,)),
         ],
         compiler_params=pltpu.CompilerParams(
             collective_id=0, has_side_effects=True, vmem_limit_bytes=56 * 2**20
@@ -553,9 +586,20 @@
         fixed_coef,
         member_coef,
         row_slot.reshape(1, rows),
-        tile_source.reshape(1, -1),
+        tile_source,
         member_tiles,
     )
+    margin, updated, grad = pl.pallas_call(
+        hand_over,
+        out_shape=(
+            jax.ShapeDtypeStruct((1, rows), F32),
+            jax.ShapeDtypeStruct((members, width), F32),
+            jax.ShapeDtypeStruct((block_count, block_width), F32),
+        ),
+        in_specs=[hbm] * 3,
+        out_specs=(hbm,) * 3,
+        scratch_shapes=[dma((3,))],
+    )(margin, updated, grad)
     return margin.reshape(rows), updated, grad
 
 

time: 105 us -> 126 us (1.20)
  Pallas kernels: 97.7 us -> 126 us
  local copies, waits for them, and re-layouts: 6.11 us -> 0 us
    pallas_call x0 -> x1, Pallas kernels: none -> 33.1 us  [body(): pl.pallas_call(hand_over, out_shape=(jax.ShapeDtypeStruct((1, rows), F32)...]
    pallas_call x1, Pallas kernels: 97.7 us -> 92.4 us  [body(): pl.pallas_call(functools.partial(kernel, dp, feat, cap), out_shape=(jax.S...]
    unnamed x3 -> x0, local copies, waits for them, and re-layouts: 4.8 us -> none
    reshape x1 -> x0, local copies, waits for them, and re-layouts: 1.31 us -> none  [body(): tile_source.reshape(1, -1)]
where the time goes in v1:
time: 126 us
  Pallas kernels  126 us (100%)
    pallas_call x1, Pallas kernels, body(): pl.pallas_call(functools.partial(kernel, dp, feat, cap), out_shape=(jax.S...  92.4 us
    pallas_call x1, Pallas kernels, body(): pl.pallas_call(hand_over, out_shape=(jax.ShapeDtypeStruct((1, rows), F32)...  33.1 us

profile of v1, /device:TPU:1, one launch (start us, length us, event | category | flops | bytes accessed | tf_op | source)
XLA Modules:
  0.0 126.2 jit_solution(5373324786097373696)
XLA Ops:
  0.6 92.4 %shard_map.112 = (f32[1,1024]{1,0:T(1,128)}, f32[4,256]{1,0:T(4,128)}, f32[512,512]{1,0:T(8,128)}) custom-call(bf16[1024,256]{1,0:T(8,128)(2,1)} %feats_hbm.1, s32[1,1024]{1,0:T(1,128)} %bitcast.5, bf16[4096,512]{1,0:T(8,128)(2,1)} %fv_hbm.1, s32[1,4096]{1,0:T(1,128)} %bitcast.4, f32[512,512]{1,0:T(8,128)} %fc_hbm.1, f32[4,256]{1,0:T(4,128)} %mcoef.1, ...), custom_call_target="tpu_custom_call" | custom-call | tf_op jit(solution)/shard_map/pallas_call | solution.py:524
  93.1 33.1 %shard_map.113 = (f32[1,1024]{1,0:T(1,128)}, f32[4,256]{1,0:T(4,128)}, f32[512,512]{1,0:T(8,128)}) custom-call(f32[1,1024]{1,0:T(1,128)} %get-tuple-element.9.margin, f32[4,256]{1,0:T(4,128)} %get-tuple-element.10.updated, f32[512,512]{1,0:T(8,128)} %get-tuple-element.11.grad), custom_call_target="tpu_custom_call" | custom-call | tf_op jit(solution)/shard_map/pallas_call | solution.py:592

commit v2 on v1

--- a/solution.py
+++ b/solution.py
@@ -84,8 +84,12 @@
     member_mask,
     acc,
     recv_c,
-    recv_rx,
-    recv_rz,
+    send_q,
+    recv_q,
+    full_q,
+    send_k,
+    recv_k,
+    full_k,
     sx,
     rx,
     sp,
@@ -98,14 +102,10 @@
     re,
     sc,
     rc,
-    srx,
-    rrx,
-    srz,
-    rrz,
-    sgz,
-    rgz,
-    sgx,
-    rgx,
+    sq,
+    rq,
+    sg,
+    rg,
     sgc,
     rgc,
     s_load,
@@ -365,18 +365,16 @@
 
     def gradient_rows(start):
         def add_chunk(q, total):
-            first_row = pl.multiple_of(q * step, step)
-            per = rows // step
-            inner = pl.multiple_of((q % per) * step, step)
-            top, low = split2(recv_e[q // per, :, pl.ds(inner, step)])
-            hot = hot_all[pl.ds(start, half), pl.ds(first_row, step)]
+            first_row = pl.multiple_of(q * rows, rows)
+            top, low = split2(recv_e[q])
+            hot = hot_all[pl.ds(start, half), pl.ds(first_row, rows)]
             weighted = jnp.concatenate([hot * top, hot * low], axis=0)
-            return total + dot_nn(weighted, fv[pl.ds(first_row, step), :])
-
-        total = lax.fori_loop(
-            0, group_rows // step, add_chunk, jnp.zeros((2 * half, block_width), F32)
+            sums = dot_nn(weighted, fv[pl.ds(first_row, rows), :])
+            return total + (sums[:half] + sums[half:])
+
+        acc[pl.ds(start, half), :] = lax.fori_loop(
+            0, feat, add_chunk, jnp.zeros((half, block_width), F32)
         )
-        acc[pl.ds(start, half), :] = total[:half] + total[half:]
 
     partner = z * plane_owners + x * cores + (1 - c)
     theirs = pl.multiple_of((1 - c) * half, half)
@@ -395,82 +393,95 @@
     core_copy.wait_recv()
     acc[pl.ds(mine, half), :] = acc[pl.ds(mine, half), :] + recv_c[...]
 
-    strip = half // chips
-    share = strip // planes
-
-    def along_x(k):
-        return (x + k) % chips
-
-    def along_z(k):
-        return (z + k) % planes
-
-    for k in range(1, chips):
-        other = along_x(k)
+    lane = planes * chips
+    me = z * chips + x
+    share_rows, share_width = half * 2 // lane, block_width // 2
+
+    def device_of(p):
+        return at((p // chips) * plane_owners + (p % chips) * cores + c)
+
+    def encode(values, codes, scales, p):
+        most = jnp.max(jnp.max(jnp.abs(values), axis=1, keepdims=True), axis=0, keepdims=True)
+        most = jnp.maximum(most, 1e-30)
+        codes[p] = jnp.round(values * (32767.0 / most)).astype(jnp.int32).astype(jnp.int16)
+        scales[p] = jnp.broadcast_to(most * (1.0 / 32767.0), (1, LANES))
+
+    def decode(codes, scales, p):
+        return codes[p].astype(jnp.int32).astype(F32) * scales[p][:, :1]
+
+    for p in range(lane):
+        rows_of = pl.ds(pl.multiple_of(mine + (p // 2) * share_rows, share_rows), share_rows)
+        values = acc[rows_of, (p % 2) * share_width : (p % 2 + 1) * share_width]
+        encode(values, send_q, send_k, p)
+
+    def send_share(k, carry):
+        p = (me + k) % lane
+        for source, target, sems in ((send_q, recv_q, 0), (send_k, recv_k, 1)):
+            pltpu.make_async_remote_copy(
+                src_ref=source.at[p],
+                dst_ref=target.at[me],
+                send_sem=sq.at[sems],
+                recv_sem=rq.at[sems],
+                device_id=device_of(p),
+                device_id_type=MESH,
+            ).start()
+        return carry
+
+    lax.fori_loop(1, lane, send_share, 0)
+    recv_q[me] = send_q[me]
+    recv_k[me] = send_k[me]
+    wait_all(recv_q.at[pl.ds(0, lane - 1)], rq.at[0])
+    wait_all(recv_k.at[pl.ds(0, lane - 1)], rq.at[1])
+    total = decode(recv_q, recv_k, 0)
+    for p in range(1, lane):
+        total = total + decode(recv_q, recv_k, p)
+    my_rows = pl.ds(pl.multiple_of(mine + (me // 2) * share_rows, share_rows), share_rows)
+    my_columns = pl.ds(pl.multiple_of((me % 2) * share_width, share_width), share_width)
+    finished = RIDGE_FIXED * fc[my_rows, my_columns] - total / dp
+    encode(finished, full_q.at[c], full_k.at[c], me)
+
+    def send_finished(k, carry):
+        p = (me + k) % lane
+        for source, sems in ((full_q, 0), (full_k, 1)):
+            pltpu.make_async_remote_copy(
+                src_ref=source.at[c, me],
+                dst_ref=source.at[c, me],
+                send_sem=sg.at[sems],
+                recv_sem=rg.at[sems],
+                device_id=device_of(p),
+                device_id_type=MESH,
+            ).start()
+        return carry
+
+    lax.fori_loop(1, lane, send_finished, 0)
+    wait_all(full_q.at[c, pl.ds(0, lane - 1)], rg.at[0])
+    wait_all(full_k.at[c, pl.ds(0, lane - 1)], rg.at[1])
+    last = [
         pltpu.make_async_remote_copy(
-            src_ref=acc.at[pl.ds(pl.multiple_of(mine + other * strip, strip), strip)],
-            dst_ref=recv_rx.at[x],
-            send_sem=srx,
-            recv_sem=rrx,
-            device_id=at(z * plane_owners + other * cores + c),
+            src_ref=source.at[c],
+            dst_ref=source.at[c],
+            send_sem=sgc.at[sems],
+            recv_sem=rgc.at[sems],
+            device_id=at(partner),
             device_id_type=MESH,
-        ).start()
-    my_strip = pl.multiple_of(mine + x * strip, strip)
-    recv_rx[x] = acc[pl.ds(my_strip, strip), :]
-    wait_all(recv_rx.at[pl.ds(0, chips - 1)], rrx)
-    total = recv_rx[0]
-    for k in range(1, chips):
-        total = total + recv_rx[k]
-    acc[pl.ds(my_strip, strip), :] = total
-    for k in range(1, planes):
-        other = along_z(k)
-        pltpu.make_async_remote_copy(
-            src_ref=acc.at[pl.ds(pl.multiple_of(my_strip + other * share, share), share)],
-            dst_ref=recv_rz.at[z],
-            send_sem=srz,
-            recv_sem=rrz,
-            device_id=at(other * plane_owners + x * cores + c),
-            device_id_type=MESH,
-        ).start()
-    my_share = pl.multiple_of(my_strip + z * share, share)
-    recv_rz[z] = acc[pl.ds(my_share, share), :]
-    wait_all(recv_rz.at[pl.ds(0, planes - 1)], rrz)
-    total = recv_rz[0]
-    for k in range(1, planes):
-        total = total + recv_rz[k]
-    grad_out[pl.ds(my_share, share), :] = (
-        RIDGE_FIXED * fc[pl.ds(my_share, share), :] - total / dp
-    )
-
-    for k in range(1, planes):
-        pltpu.make_async_remote_copy(
-            src_ref=grad_out.at[pl.ds(my_share, share)],
-            dst_ref=grad_out.at[pl.ds(my_share, share)],
-            send_sem=sgz,
-            recv_sem=rgz,
-            device_id=at(along_z(k) * plane_owners + x * cores + c),
-            device_id_type=MESH,
-        ).start()
-    wait_all(grad_out.at[pl.ds(0, (planes - 1) * share)], rgz)
-    for k in range(1, chips):
-        pltpu.make_async_remote_copy(
-            src_ref=grad_out.at[pl.ds(my_strip, strip)],
-            dst_ref=grad_out.at[pl.ds(my_strip, strip)],
-            send_sem=sgx,
-            recv_sem=rgx,
-            device_id=at(z * plane_owners + along_x(k) * cores + c),
-            device_id_type=MESH,
-        ).start()
-    wait_all(grad_out.at[pl.ds(0, (chips - 1) * strip)], rgx)
-    last = pltpu.make_async_remote_copy(
-        src_ref=grad_out.at[pl.ds(mine, half)],
-        dst_ref=grad_out.at[pl.ds(mine, half)],
-        send_sem=sgc,
-        recv_sem=rgc,
-        device_id=at(partner),
-        device_id_type=MESH,
-    )
-    last.start()
-    last.wait()
+        )
+        for source, sems in ((full_q, 0), (full_k, 1))
+    ]
+    for copy in last:
+        copy.start()
+
+    def write_half(core):
+        for p in range(lane):
+            first_row = core * half + (p // 2) * share_rows
+            grad_out[
+                pl.ds(pl.multiple_of(first_row, share_rows), share_rows),
+                (p % 2) * share_width : (p % 2 + 1) * share_width,
+            ] = decode(full_q.at[core], full_k.at[core], p)
+
+    write_half(c)
+    for copy in last:
+        copy.wait()
+    write_half(1 - c)
 
     wait_all(send_x.at[pl.ds(0, dp - 1)], sx)
     wait_all(send_p.at[pl.ds(0, feat - 1)], sp)
@@ -479,23 +490,16 @@
     for k in range(1, feat):
         wait_all(send_e, se.at[k - 1])
     core_copy.wait_send()
-    wait_all(recv_rx.at[pl.ds(0, chips - 1)], srx)
-    wait_all(recv_rz.at[pl.ds(0, planes - 1)], srz)
-    wait_all(grad_out.at[pl.ds(0, (planes - 1) * share)], sgz)
-    wait_all(grad_out.at[pl.ds(0, (chips - 1) * strip)], sgx)
-
-
-def hand_over(margin, updated, grad, margin_out, updated_out, grad_out, sems):
-    copies = [
-        pltpu.make_async_copy(source, target, sems.at[k])
-        for k, (source, target) in enumerate(
-            ((grad, grad_out), (updated, updated_out), (margin, margin_out))
-        )
-    ]
-    for copy in copies:
-        copy.start()
-    for copy in copies:
-        copy.wait()
+    wait_all(send_q.at[pl.ds(0, lane - 1)], sq.at[0])
+    wait_all(send_k.at[pl.ds(0, lane - 1)], sq.at[1])
+    wait_all(full_q.at[c, pl.ds(0, lane - 1)], sg.at[0])
+    wait_all(full_k.at[c, pl.ds(0, lane - 1)], sg.at[1])
+
+
+def hand_over(margin, updated, grad, margin_out, updated_out, grad_out):
+    margin_out[...] = margin[...]
+    updated_out[...] = updated[...]
+    grad_out[...] = grad[...]
 
 
 def body(
@@ -517,6 +521,8 @@
     block_count, block_width = fixed_coef.shape
     cap = 2 * rows // dp
     half = block_count // cores
+    lane = planes * chips
+    share = (half * 2 // lane, block_width // 2)
     vmem = pl.BlockSpec(memory_space=pltpu.VMEM)
     hbm = pl.BlockSpec(memory_space=pl.ANY)
     smem = pl.BlockSpec(memory_space=pltpu.SMEM)
@@ -549,8 +555,12 @@
             pltpu.VMEM((members, dp * cap), F32),
             pltpu.VMEM((block_count, block_width), F32),
             pltpu.VMEM((half, block_width), F32),
-            pltpu.VMEM((chips, half // chips, block_width), F32),
-            pltpu.VMEM((planes, half // chips // planes, block_width), F32),
+            pltpu.VMEM((lane, *share), jnp.int16),
+            pltpu.VMEM((lane, *share), jnp.int16),
+            pltpu.VMEM((cores, lane, *share), jnp.int16),
+            pltpu.VMEM((lane, 1, LANES), F32),
+            pltpu.VMEM((lane, 1, LANES), F32),
+            pltpu.VMEM((cores, lane, 1, LANES), F32),
             dma,
             dma,
             dma,
@@ -563,16 +573,12 @@
             dma,
             dma,
             dma,
-            dma,
-            dma,
-            dma,
-            dma,
-            dma,
-            dma,
-            dma,
-            dma,
-            dma,
-            dma,
+            dma((2,)),
+            dma((2,)),
+            dma((2,)),
+            dma((2,)),
+            dma((2,)),
+            dma((2,)),
             dma((3,)),
         ],
         compiler_params=pltpu.CompilerParams(
@@ -596,9 +602,8 @@
             jax.ShapeDtypeStruct((members, width), F32),
             jax.ShapeDtypeStruct((block_count, block_width), F32),
         ),
-        in_specs=[hbm] * 3,
-        out_specs=(hbm,) * 3,
-        scratch_shapes=[dma((3,))],
+        in_specs=[vmem] * 3,
+        out_specs=(vmem,) * 3,
     )(margin, updated, grad)
     return margin.reshape(rows), updated, grad
 

time: 126 us -> 85.6 us (0.68)
  Pallas kernels: 126 us -> 84.8 us
    pallas_call x1, Pallas kernels: 33.1 us -> 2.27 us  [body(): pl.pallas_call(hand_over, out_shape=(jax.ShapeDtypeStruct((1, rows), F32)...]
    pallas_call x1, Pallas kernels: 92.4 us -> 82.6 us  [body(): pl.pallas_call(functools.partial(kernel, dp, feat, cap), out_shape=(jax.S...]
where the time goes in v2:
time: 85.6 us; the launch traced here: 85.5 us
  Pallas kernels  84.8 us (99%)
    pallas_call x1, Pallas kernels, body(): pl.pallas_call(functools.partial(kernel, dp, feat, cap), out_shape=(jax.S...  82.6 us
    pallas_call x1, Pallas kernels, body(): pl.pallas_call(hand_over, out_shape=(jax.ShapeDtypeStruct((1, rows), F32)...  2.27 us

profile of v2, /device:TPU:1, one launch (start us, length us, event | category | flops | bytes accessed | tf_op | source)
XLA Modules:
  0.0 85.5 jit_solution(9664898476026521011)
XLA Ops:
  0.6 82.6 %shard_map.112 = (f32[1,1024]{1,0:T(1,128)}, f32[4,256]{1,0:T(4,128)}, f32[512,512]{1,0:T(8,128)}) custom-call(bf16[1024,256]{1,0:T(8,128)(2,1)} %feats_hbm.1, s32[1,1024]{1,0:T(1,128)} %bitcast.5, bf16[4096,512]{1,0:T(8,128)(2,1)} %fv_hbm.1, s32[1,4096]{1,0:T(1,128)} %bitcast.4, f32[512,512]{1,0:T(8,128)} %fc_hbm.1, f32[4,256]{1,0:T(4,128)} %mcoef.1, ...), custom_call_target="tpu_custom_call" | custom-call | tf_op jit(solution)/shard_map/pallas_call | solution.py:530
  83.2 2.3 %shard_map.113 = (f32[1,1024]{1,0:T(1,128)}, f32[4,256]{1,0:T(4,128)}, f32[512,512]{1,0:T(8,128)}) custom-call(f32[1,1024]{1,0:T(1,128)} %get-tuple-element.9.margin, f32[4,256]{1,0:T(4,128)} %get-tuple-element.10.updated, f32[512,512]{1,0:T(8,128)} %get-tuple-element.11.grad), custom_call_target="tpu_custom_call" | custom-call | tf_op jit(solution)/shard_map/pallas_call | solution.py:598

commit v3 on v2

--- a/solution.py
+++ b/solution.py
@@ -44,6 +44,11 @@
 
 def as_f32(mask):
     return jnp.where(mask, 1.0, 0.0).astype(F32)
+
+
+def decode(codes, scale):
+    values = codes.astype(jnp.int32).astype(F32)
+    return values * jnp.concatenate([scale] * (values.shape[1] // LANES), axis=1)
 
 
 def grid_of(dp):
@@ -65,7 +70,8 @@
     mtiles,
     margin_out,
     coef_out,
-    grad_out,
+    full_q,
+    full_k,
     feats,
     fv,
     fc,
@@ -86,10 +92,8 @@
     recv_c,
     send_q,
     recv_q,
-    full_q,
     send_k,
     recv_k,
-    full_k,
     sx,
     rx,
     sp,
@@ -242,6 +246,7 @@
             widened[m * cap : (m + 1) * cap] * slot_mask, axis=0, keepdims=True
         )
 
+    share_of = LANES // cap
     owner_hot = as_bf16((slot_row >> cap_bits) == iota((dp, rows), 0))
     slot_hot = as_f32((slot_row & (cap - 1)) == iota((cap, rows), 0))
     label_row = labels[...].astype(F32)
@@ -273,15 +278,16 @@
 
     lax.fori_loop(1, dp, send_score, 0)
     recv_s[i] = send_s[i]
-    wait_all(recv_x.at[pl.ds(0, dp - 1)], rx)
     wait_all(recv_s.at[pl.ds(0, dp - 1)], rs)
-
-    mask = member_mask[...]
-    got = recv_x[...].reshape(slots, feats.shape[1])
     arrived = recv_s[...].reshape(dp, LANES)[:, : 2 * cap].astype(BF16)
     expanded = dot_tn(arrived, spread)
     score_row = jnp.sum(expanded[:cap] * slot_mask, axis=0, keepdims=True)
     answer_row = jnp.sum(expanded[cap:] * slot_mask, axis=0, keepdims=True)
+    mask = member_mask[...]
+    lane_hot = as_f32((slot_row & (cap - 1)) + (i % share_of) * cap == iota((LANES, rows), 0))
+    wait_all(recv_x.at[pl.ds(0, dp - 1)], rx)
+
+    got = recv_x[...].reshape(slots, feats.shape[1])
 
     def project(vectors):
         top, low = split2(vectors)
@@ -321,16 +327,14 @@
     updated = coef + step_sum
     coef_out[...] = updated
 
-    new_top, new_low = split2(project(updated))
-    stacked = jnp.concatenate([spread * new_top, spread * new_low], axis=0)
-    slot_wide = as_bf16((iota((LANES, slots), 1) & (cap - 1)) == iota((LANES, slots), 0))
-    folded = dot_nt(stacked, slot_wide)
-    send_r[...] = (folded[:dp] + folded[dp:]).reshape(dp, 1, LANES)
+    new_scores = project(updated)
+    for k in range(slots // LANES):
+        send_r[k] = new_scores[:, k * LANES : (k + 1) * LANES]
 
     def send_back(k, carry):
         sender = (i + k) % dp
         pltpu.make_async_remote_copy(
-            src_ref=send_r.at[sender],
+            src_ref=send_r.at[sender // share_of],
             dst_ref=recv_r.at[i],
             send_sem=sr,
             recv_sem=rr,
@@ -340,11 +344,11 @@
         return carry
 
     lax.fori_loop(1, dp, send_back, 0)
-    recv_r[i] = send_r[i]
+    recv_r[i] = send_r[i // share_of]
     wait_all(recv_r.at[pl.ds(0, dp - 1)], rr)
-    back_top, back_low = split2(recv_r[...].reshape(dp, LANES)[:, :cap])
+    back_top, back_low = split2(recv_r[...].reshape(dp, LANES))
     looked = dot_tn(back_top, owner_hot) + dot_tn(back_low, owner_hot)
-    member_score = jnp.sum(looked * slot_hot, axis=0, keepdims=True)
+    member_score = jnp.sum(looked * lane_hot, axis=0, keepdims=True)
     margin = fixed_score + member_score
     margin_out[...] = margin
     send_e[...] = label_row - 1.0 / (1.0 + jnp.exp(-margin))
@@ -359,21 +363,26 @@
             device_id_type=MESH,
         ).start()
     recv_e[f] = send_e[...]
+
+    half = block_count // cores
+
+    def quarter(q, start, count):
+        first_row = pl.multiple_of(q * rows, rows)
+        top, low = split2(recv_e[q])
+        hot = hot_all[pl.ds(start, count), pl.ds(first_row, rows)]
+        weighted = jnp.concatenate([hot * top, hot * low], axis=0)
+        sums = dot_nn(weighted, fv[pl.ds(first_row, rows), :])
+        return sums[:count] + sums[count:]
+
+    acc[...] = quarter(f, 0, block_count)
     wait_all(recv_e.at[pl.ds(0, feat - 1)], re)
 
-    half = block_count // cores
-
     def gradient_rows(start):
-        def add_chunk(q, total):
-            first_row = pl.multiple_of(q * rows, rows)
-            top, low = split2(recv_e[q])
-            hot = hot_all[pl.ds(start, half), pl.ds(first_row, rows)]
-            weighted = jnp.concatenate([hot * top, hot * low], axis=0)
-            sums = dot_nn(weighted, fv[pl.ds(first_row, rows), :])
-            return total + (sums[:half] + sums[half:])
-
         acc[pl.ds(start, half), :] = lax.fori_loop(
-            0, feat, add_chunk, jnp.zeros((half, block_width), F32)
+            1,
+            feat,
+            lambda k, total: total + quarter((f + k) % feat, start, half),
+            acc[pl.ds(start, half), :],
         )
 
     partner = z * plane_owners + x * cores + (1 - c)
@@ -406,9 +415,6 @@
         codes[p] = jnp.round(values * (32767.0 / most)).astype(jnp.int32).astype(jnp.int16)
         scales[p] = jnp.broadcast_to(most * (1.0 / 32767.0), (1, LANES))
 
-    def decode(codes, scales, p):
-        return codes[p].astype(jnp.int32).astype(F32) * scales[p][:, :1]
-
     for p in range(lane):
         rows_of = pl.ds(pl.multiple_of(mine + (p // 2) * share_rows, share_rows), share_rows)
         values = acc[rows_of, (p % 2) * share_width : (p % 2 + 1) * share_width]
@@ -432,20 +438,25 @@
     recv_k[me] = send_k[me]
     wait_all(recv_q.at[pl.ds(0, lane - 1)], rq.at[0])
     wait_all(recv_k.at[pl.ds(0, lane - 1)], rq.at[1])
-    total = decode(recv_q, recv_k, 0)
+    total = decode(recv_q[0], recv_k[0])
     for p in range(1, lane):
-        total = total + decode(recv_q, recv_k, p)
+        total = total + decode(recv_q[p], recv_k[p])
     my_rows = pl.ds(pl.multiple_of(mine + (me // 2) * share_rows, share_rows), share_rows)
     my_columns = pl.ds(pl.multiple_of((me % 2) * share_width, share_width), share_width)
     finished = RIDGE_FIXED * fc[my_rows, my_columns] - total / dp
+    wait_all(send_q.at[pl.ds(0, lane - 1)], sq.at[0])
+    wait_all(send_k.at[pl.ds(0, lane - 1)], sq.at[1])
     encode(finished, full_q.at[c], full_k.at[c], me)
+    for p in range(lane):
+        send_q[p] = full_q[c, me]
+        send_k[p] = full_k[c, me]
 
     def send_finished(k, carry):
         p = (me + k) % lane
-        for source, sems in ((full_q, 0), (full_k, 1)):
+        for source, target, sems in ((send_q, full_q, 0), (send_k, full_k, 1)):
             pltpu.make_async_remote_copy(
-                src_ref=source.at[c, me],
-                dst_ref=source.at[c, me],
+                src_ref=source.at[p],
+                dst_ref=target.at[c, me],
                 send_sem=sg.at[sems],
                 recv_sem=rg.at[sems],
                 device_id=device_of(p),
@@ -470,36 +481,31 @@
     for copy in last:
         copy.start()
 
-    def write_half(core):
-        for p in range(lane):
-            first_row = core * half + (p // 2) * share_rows
-            grad_out[
-                pl.ds(pl.multiple_of(first_row, share_rows), share_rows),
-                (p % 2) * share_width : (p % 2 + 1) * share_width,
-            ] = decode(full_q.at[core], full_k.at[core], p)
-
-    write_half(c)
     for copy in last:
         copy.wait()
-    write_half(1 - c)
 
     wait_all(send_x.at[pl.ds(0, dp - 1)], sx)
     wait_all(send_p.at[pl.ds(0, feat - 1)], sp)
     wait_all(send_s.at[pl.ds(0, dp - 1)], ss)
-    wait_all(send_r.at[pl.ds(0, dp - 1)], sr)
+    wait_all(recv_r.at[pl.ds(0, dp - 1)], sr)
     for k in range(1, feat):
         wait_all(send_e, se.at[k - 1])
     core_copy.wait_send()
-    wait_all(send_q.at[pl.ds(0, lane - 1)], sq.at[0])
-    wait_all(send_k.at[pl.ds(0, lane - 1)], sq.at[1])
-    wait_all(full_q.at[c, pl.ds(0, lane - 1)], sg.at[0])
-    wait_all(full_k.at[c, pl.ds(0, lane - 1)], sg.at[1])
-
-
-def hand_over(margin, updated, grad, margin_out, updated_out, grad_out):
+    wait_all(send_q.at[pl.ds(0, lane - 1)], sg.at[0])
+    wait_all(send_k.at[pl.ds(0, lane - 1)], sg.at[1])
+
+
+def write_outputs(margin, updated, codes, scales, margin_out, updated_out, grad_out):
     margin_out[...] = margin[...]
     updated_out[...] = updated[...]
-    grad_out[...] = grad[...]
+    cores, lane, share_rows, share_width = codes.shape
+    for core in range(cores):
+        for p in range(lane):
+            first_row = (core * lane // 2 + p // 2) * share_rows
+            grad_out[
+                first_row : first_row + share_rows,
+                (p % 2) * share_width : (p % 2 + 1) * share_width,
+            ] = decode(codes[core, p], scales[core, p])
 
 
 def body(
@@ -527,15 +533,16 @@
     hbm = pl.BlockSpec(memory_space=pl.ANY)
     smem = pl.BlockSpec(memory_space=pltpu.SMEM)
     dma = pltpu.SemaphoreType.DMA
-    margin, updated, grad = pl.pallas_call(
+    margin, updated, codes, scales = pl.pallas_call(
         functools.partial(kernel, dp, feat, cap),
         out_shape=(
             jax.ShapeDtypeStruct((1, rows), F32),
             jax.ShapeDtypeStruct((members, width), F32),
-            jax.ShapeDtypeStruct((block_count, block_width), F32),
+            jax.ShapeDtypeStruct((cores, lane, *share), jnp.int16),
+            jax.ShapeDtypeStruct((cores, lane, 1, LANES), F32),
         ),
         in_specs=[hbm, vmem, hbm, vmem, hbm, vmem, vmem, vmem, smem],
-        out_specs=(vmem, vmem, vmem),
+        out_specs=(vmem,) * 4,
         scratch_shapes=[
             pltpu.VMEM((rows, width), BF16),
             pltpu.VMEM(fixed_values.shape, BF16),
@@ -547,7 +554,7 @@
             pltpu.VMEM((feat, 1, rows), F32),
             pltpu.VMEM((dp, 1, LANES), F32),
             pltpu.VMEM((dp, 1, LANES), F32),
-            pltpu.VMEM((dp, 1, LANES), F32),
+            pltpu.VMEM((dp * cap // LANES, 1, LANES), F32),
             pltpu.VMEM((dp, 1, LANES), F32),
             pltpu.VMEM((1, rows), F32),
             pltpu.VMEM((feat, 1, rows), F32),
@@ -557,10 +564,8 @@
             pltpu.VMEM((half, block_width), F32),
             pltpu.VMEM((lane, *share), jnp.int16),
             pltpu.VMEM((lane, *share), jnp.int16),
-            pltpu.VMEM((cores, lane, *share), jnp.int16),
             pltpu.VMEM((lane, 1, LANES), F32),
             pltpu.VMEM((lane, 1, LANES), F32),
-            pltpu.VMEM((cores, lane, 1, LANES), F32),
             dma,
             dma,
             dma,
@@ -596,15 +601,15 @@
         member_tiles,
     )
     margin, updated, grad = pl.pallas_call(
-        hand_over,
+        write_outputs,
         out_shape=(
             jax.ShapeDtypeStruct((1, rows), F32),
             jax.ShapeDtypeStruct((members, width), F32),
             jax.ShapeDtypeStruct((block_count, block_width), F32),
         ),
-        in_specs=[vmem] * 3,
+        in_specs=[vmem] * 4,
         out_specs=(vmem,) * 3,
-    )(margin, updated, grad)
+    )(margin, updated, codes, scales)
     return margin.reshape(rows), updated, grad
 
 

time: 85.6 us -> 85.1 us (level)
  no operation moved by 1% of the time
where the time goes in v3:
time: 85.1 us; the launch traced here: 85 us
  Pallas kernels  84.3 us (99%)
    pallas_call x1, Pallas kernels, body(): pl.pallas_call(functools.partial(kernel, dp, feat, cap), out_shape=(jax.S...  82.2 us
    pallas_call x1, Pallas kernels, body(): pl.pallas_call(write_outputs, out_shape=(jax.ShapeDtypeStruct((1, rows),...  2.13 us

profile of v3, /device:TPU:1, one launch (start us, length us, event | category | flops | bytes accessed | tf_op | source)
XLA Modules:
  0.0 85.0 jit_solution(9048089500773932359)
XLA Ops:
  0.6 82.2 %shard_map.112 = (f32[1,1024]{1,0:T(1,128)}, f32[4,256]{1,0:T(4,128)}, s16[2,32,16,256]{3,2,1,0:T(8,128)(2,1)}, f32[2,32,1,128]{3,2,1,0:T(1,128)}) custom-call(bf16[1024,256]{1,0:T(8,128)(2,1)} %feats_hbm.1, s32[1,1024]{1,0:T(1,128)} %bitcast.5, bf16[4096,512]{1,0:T(8,128)(2,1)} %fv_hbm.1, s32[1,4096]{1,0:T(1,128)} %bitcast.4, f32[512,512]{1,0:T(8,128)} %fc_hbm.1, ...), custom_call_target="tpu_custom_call" | custom-call | tf_op jit(solution)/shard_map/pallas_call | solution.py:536
  82.9 2.1 %shard_map.113 = (f32[1,1024]{1,0:T(1,128)}, f32[4,256]{1,0:T(4,128)}, f32[512,512]{1,0:T(8,128)}) custom-call(f32[1,1024]{1,0:T(1,128)} %get-tuple-element.10.margin, f32[4,256]{1,0:T(4,128)} %get-tuple-element.11.updated, s16[2,32,16,256]{3,2,1,0:T(8,128)(2,1)} %get-tuple-element.12.codes, f32[2,32,1,128]{3,2,1,0:T(1,128)} %get-tuple-element.13.scales), custom_call_target="tpu_custom_call" | custom-call | tf_op jit(solution)/shard_map/pallas_call | solution.py:603

commit v4 on v3

--- a/solution.py
+++ b/solution.py
@@ -10,6 +10,7 @@
 CG_ITERS = 2
 TILE = 128
 LANES = 128
+STRIDE = 13
 RIDGE_MEMBER = 1.0
 RIDGE_FIXED = 1.0
 F32 = jnp.float32
@@ -421,8 +422,8 @@
         encode(values, send_q, send_k, p)
 
     def send_share(k, carry):
-        p = (me + k) % lane
-        for source, target, sems in ((send_q, recv_q, 0), (send_k, recv_k, 1)):
+        p = (me + STRIDE * k) % lane
+        for source, target, sems in ((send_k, recv_k, 1), (send_q, recv_q, 0)):
             pltpu.make_async_remote_copy(
                 src_ref=source.at[p],
                 dst_ref=target.at[me],
@@ -444,19 +445,14 @@
     my_rows = pl.ds(pl.multiple_of(mine + (me // 2) * share_rows, share_rows), share_rows)
     my_columns = pl.ds(pl.multiple_of((me % 2) * share_width, share_width), share_width)
     finished = RIDGE_FIXED * fc[my_rows, my_columns] - total / dp
-    wait_all(send_q.at[pl.ds(0, lane - 1)], sq.at[0])
-    wait_all(send_k.at[pl.ds(0, lane - 1)], sq.at[1])
     encode(finished, full_q.at[c], full_k.at[c], me)
-    for p in range(lane):
-        send_q[p] = full_q[c, me]
-        send_k[p] = full_k[c, me]
 
     def send_finished(k, carry):
-        p = (me + k) % lane
-        for source, target, sems in ((send_q, full_q, 0), (send_k, full_k, 1)):
+        p = (me + STRIDE * k) % lane
+        for source, sems in ((full_k, 1), (full_q, 0)):
             pltpu.make_async_remote_copy(
-                src_ref=source.at[p],
-                dst_ref=target.at[c, me],
+                src_ref=source.at[c, me],
+                dst_ref=source.at[c, me],
                 send_sem=sg.at[sems],
                 recv_sem=rg.at[sems],
                 device_id=device_of(p),
@@ -491,6 +487,8 @@
     for k in range(1, feat):
         wait_all(send_e, se.at[k - 1])
     core_copy.wait_send()
+    wait_all(send_q.at[pl.ds(0, lane - 1)], sq.at[0])
+    wait_all(send_k.at[pl.ds(0, lane - 1)], sq.at[1])
     wait_all(send_q.at[pl.ds(0, lane - 1)], sg.at[0])
     wait_all(send_k.at[pl.ds(0, lane - 1)], sg.at[1])
 

time: 85.1 us -> 83.5 us (0.981)
  Pallas kernels: 84.3 us -> 82.7 us
    pallas_call x1, Pallas kernels: 82.2 us -> 80.5 us  [body(): pl.pallas_call(functools.partial(kernel, dp, feat, cap), out_shape=(jax.S...]
where the time goes in v4:
time: 83.5 us; the launch traced here: 83.3 us
  Pallas kernels  82.7 us (99%)
    pallas_call x1, Pallas kernels, body(): pl.pallas_call(functools.partial(kernel, dp, feat, cap), out_shape=(jax.S...  80.5 us
    pallas_call x1, Pallas kernels, body(): pl.pallas_call(write_outputs, out_shape=(jax.ShapeDtypeStruct((1, rows),...  2.13 us

profile of v4, /device:TPU:1, one launch (start us, length us, event | category | flops | bytes accessed | tf_op | source)
XLA Modules:
  0.0 83.3 jit_solution(6394711737158721833)
XLA Ops:
  0.6 80.5 %shard_map.112 = (f32[1,1024]{1,0:T(1,128)}, f32[4,256]{1,0:T(4,128)}, s16[2,32,16,256]{3,2,1,0:T(8,128)(2,1)}, f32[2,32,1,128]{3,2,1,0:T(1,128)}) custom-call(bf16[1024,256]{1,0:T(8,128)(2,1)} %feats_hbm.1, s32[1,1024]{1,0:T(1,128)} %bitcast.5, bf16[4096,512]{1,0:T(8,128)(2,1)} %fv_hbm.1, s32[1,4096]{1,0:T(1,128)} %bitcast.4, f32[512,512]{1,0:T(8,128)} %fc_hbm.1, ...), custom_call_target="tpu_custom_call" | custom-call | tf_op jit(solution)/shard_map/pallas_call | solution.py:534
  81.2 2.1 %shard_map.113 = (f32[1,1024]{1,0:T(1,128)}, f32[4,256]{1,0:T(4,128)}, f32[512,512]{1,0:T(8,128)}) custom-call(f32[1,1024]{1,0:T(1,128)} %get-tuple-element.10.margin, f32[4,256]{1,0:T(4,128)} %get-tuple-element.11.updated, s16[2,32,16,256]{3,2,1,0:T(8,128)(2,1)} %get-tuple-element.12.codes, f32[2,32,1,128]{3,2,1,0:T(1,128)} %get-tuple-element.13.scales), custom_call_target="tpu_custom_call" | custom-call | tf_op jit(solution)/shard_map/pallas_call | solution.py:601

commit v5 on v4

--- a/solution.py
+++ b/solution.py
@@ -89,6 +89,7 @@
     recv_e,
     coef_parts,
     member_mask,
+    side,
     acc,
     recv_c,
     send_q,
@@ -169,23 +170,23 @@
     lax.fori_loop(0, planes, pick_plane, 0)
     pl.semaphore_wait(barrier, dp - 1 + feat - 1)
 
-    def send_feats(owner):
+    def send_feats(owner, k):
         pltpu.make_async_remote_copy(
             src_ref=send_x.at[owner],
             dst_ref=recv_x.at[i],
             send_sem=sx,
-            recv_sem=rx,
+            recv_sem=rx.at[k],
             device_id=at(owner),
             device_id_type=MESH,
         ).start()
 
     def send_far(q, carry):
         for k in sorted(range(1, planes), key=lambda k: -min(k, planes - k)):
-            send_feats(((z + k) % planes) * plane_owners + (i + q) % plane_owners)
+            send_feats(((z + k) % planes) * plane_owners + (i + q) % plane_owners, k)
         return carry
 
     def send_near(q, carry):
-        send_feats(z * plane_owners + (i + q) % plane_owners)
+        send_feats(z * plane_owners + (i + q) % plane_owners, 0)
         return carry
 
     lax.fori_loop(0, plane_owners, send_far, 0)
@@ -282,13 +283,40 @@
     wait_all(recv_s.at[pl.ds(0, dp - 1)], rs)
     arrived = recv_s[...].reshape(dp, LANES)[:, : 2 * cap].astype(BF16)
     expanded = dot_tn(arrived, spread)
-    score_row = jnp.sum(expanded[:cap] * slot_mask, axis=0, keepdims=True)
-    answer_row = jnp.sum(expanded[cap:] * slot_mask, axis=0, keepdims=True)
+    side[0:1, :] = jnp.sum(expanded[:cap] * slot_mask, axis=0, keepdims=True)
+    side[1:2, :] = jnp.sum(expanded[cap:] * slot_mask, axis=0, keepdims=True)
     mask = member_mask[...]
     lane_hot = as_f32((slot_row & (cap - 1)) + (i % share_of) * cap == iota((LANES, rows), 0))
-    wait_all(recv_x.at[pl.ds(0, dp - 1)], rx)
+    coef = mcoef[...]
+    coef_stack = jnp.concatenate(split2(coef), axis=0)
+    gradient = -RIDGE_MEMBER * coef
+    diagonal = jnp.full(coef.shape, RIDGE_MEMBER, F32)
+    for k in sorted(range(planes), key=lambda k: min(k, planes - k)):
+        wait_all(recv_x.at[pl.ds(0, plane_owners - (k == 0))], rx.at[k])
+        plane = (z - k + planes) % planes
+        span = pl.ds(pl.multiple_of(plane * plane_slots, plane_slots), plane_slots)
+        block = recv_x[pl.ds(plane * plane_owners, plane_owners)]
+        block = block.reshape(plane_slots, feats.shape[1])
+        here = member_mask[:, span]
+        dots = dot_nt(coef_stack, block)
+        logit = side[0:1, span] + jnp.sum(
+            (dots[:members] + dots[members:]) * here, axis=0, keepdims=True
+        )
+        probability = 1.0 / (1.0 + jnp.exp(-logit))
+        slope = probability * (1.0 - probability)
+        side[2:3, span] = slope
+        left = jnp.concatenate(split2(here * (side[1:2, span] - probability)), axis=0)
+        sums = dot_nn(left, block)
+        gradient = gradient + (sums[:members] + sums[members:])
+        wide = block.astype(F32)
+        square_top, square_low = split2(wide * wide)
+        slope_top, slope_low = split2(here * slope)
+        first = dot_nn(jnp.concatenate([slope_top, slope_low], axis=0), square_top)
+        second = dot_nn(slope_top, square_low)
+        diagonal = diagonal + (first[:members] + first[members:] + second)
 
     got = recv_x[...].reshape(slots, feats.shape[1])
+    weight = side[2:3, :]
 
     def project(vectors):
         top, low = split2(vectors)
@@ -300,16 +328,6 @@
         sums = dot_nn(jnp.concatenate([top, low], axis=0), got)
         return sums[:members] + sums[members:]
 
-    coef = mcoef[...]
-    probability = 1.0 / (1.0 + jnp.exp(-(score_row + project(coef))))
-    weight = probability * (1.0 - probability)
-    gradient = gather_rows(answer_row - probability) - RIDGE_MEMBER * coef
-    got_wide = got.astype(F32)
-    square_top, square_low = split2(got_wide * got_wide)
-    weight_top, weight_low = split2(mask * weight)
-    first = dot_nn(jnp.concatenate([weight_top, weight_low], axis=0), square_top)
-    second = dot_nn(weight_top, square_low)
-    diagonal = first[:members] + first[members:] + second + RIDGE_MEMBER
     step_sum = jnp.zeros_like(coef)
     remain = gradient
     scaled = remain / diagonal
@@ -379,12 +397,10 @@
     wait_all(recv_e.at[pl.ds(0, feat - 1)], re)
 
     def gradient_rows(start):
-        acc[pl.ds(start, half), :] = lax.fori_loop(
-            1,
-            feat,
-            lambda k, total: total + quarter((f + k) % feat, start, half),
-            acc[pl.ds(start, half), :],
-        )
+        total = acc[pl.ds(start, half), :]
+        for k in range(1, feat):
+            total = total + quarter((f + k) % feat, start, half)
+        acc[pl.ds(start, half), :] = total
 
     partner = z * plane_owners + x * cores + (1 - c)
     theirs = pl.multiple_of((1 - c) * half, half)
@@ -558,6 +574,7 @@
             pltpu.VMEM((feat, 1, rows), F32),
             pltpu.VMEM((2 * block_count, block_width), BF16),
             pltpu.VMEM((members, dp * cap), F32),
+            pltpu.VMEM((3, dp * cap), F32),
             pltpu.VMEM((block_count, block_width), F32),
             pltpu.VMEM((half, block_width), F32),
             pltpu.VMEM((lane, *share), jnp.int16),
@@ -565,7 +582,7 @@
             pltpu.VMEM((lane, 1, LANES), F32),
             pltpu.VMEM((lane, 1, LANES), F32),
             dma,
-            dma,
+            dma((planes,)),
             dma,
             dma,
             dma,

time: 83.5 us -> 85.6 us (1.025)
  Pallas kernels: 82.7 us -> 84.8 us
    pallas_call x1, Pallas kernels: 80.5 us -> 82.7 us  [body(): pl.pallas_call(functools.partial(kernel, dp, feat, cap), out_shape=(jax.S...]
where the time goes in v5:
time: 85.6 us; the launch traced here: 85.5 us
  Pallas kernels  84.8 us (99%)
    pallas_call x1, Pallas kernels, body(): pl.pallas_call(functools.partial(kernel, dp, feat, cap), out_shape=(jax.S...  82.7 us
    pallas_call x1, Pallas kernels, body(): pl.pallas_call(write_outputs, out_shape=(jax.ShapeDtypeStruct((1, rows),...  2.13 us

profile of v5, /device:TPU:1, one launch (start us, length us, event | category | flops | bytes accessed | tf_op | source)
XLA Modules:
  0.0 85.5 jit_solution(14480414926248749489)
XLA Ops:
  0.6 82.7 %shard_map.112 = (f32[1,1024]{1,0:T(1,128)}, f32[4,256]{1,0:T(4,128)}, s16[2,32,16,256]{3,2,1,0:T(8,128)(2,1)}, f32[2,32,1,128]{3,2,1,0:T(1,128)}) custom-call(bf16[1024,256]{1,0:T(8,128)(2,1)} %feats_hbm.1, s32[1,1024]{1,0:T(1,128)} %bitcast.5, bf16[4096,512]{1,0:T(8,128)(2,1)} %fv_hbm.1, s32[1,4096]{1,0:T(1,128)} %bitcast.4, f32[512,512]{1,0:T(8,128)} %fc_hbm.1, ...), custom_call_target="tpu_custom_call" | custom-call | tf_op jit(solution)/shard_map/pallas_call | solution.py:550
  83.3 2.1 %shard_map.113 = (f32[1,1024]{1,0:T(1,128)}, f32[4,256]{1,0:T(4,128)}, f32[512,512]{1,0:T(8,128)}) custom-call(f32[1,1024]{1,0:T(1,128)} %get-tuple-element.10.margin, f32[4,256]{1,0:T(4,128)} %get-tuple-element.11.updated, s16[2,32,16,256]{3,2,1,0:T(8,128)(2,1)} %get-tuple-element.12.codes, f32[2,32,1,128]{3,2,1,0:T(1,128)} %get-tuple-element.13.scales), custom_call_target="tpu_custom_call" | custom-call | tf_op jit(solution)/shard_map/pallas_call | solution.py:618
